TPU v7x, 32 devices: a whole 2x2x4 slice. The times are simulated.
32 devices in a mesh: span: 4 (over z), grp: 8 (over y, x, core).
Axes of the slice: x: 2, y: 2, z: 4, core: 2. Of those that a mesh axis runs over, the one named last changes fastest.
Arguments:
- displacement: float32 [4, 5, 8192], P('span', None, 'grp'), may hold values from -3 to 3
- velocity: float32 [4, 5, 8192], P('span', None, 'grp'), may hold values from -3 to 3
- nodal_load: float32 [4, 5, 8192], P('span', None, 'grp'), may hold values from -6 to 6
- nodal_mass: float32 [4, 8192], P('span', 'grp'), may hold values from 1 to 4
- plastic_strain: float32 [4, 128, 3, 5, 128], P('span', 'grp'), may hold values from -0.3 to 0.3
- hardening: float32 [4, 128, 5, 128], P('span', 'grp'), may hold values from 0 to 0.2
- ply_modulus: float32 [4, 128, 5, 128], P('span', 'grp'), may hold values from 0.5 to 2
- inverse_size: float32 [4, 128, 128], P('span', 'grp'), may hold values from 0.5 to 2
- cost_map: int32 [4, 128], P('span'), may hold values from 1 to 4
- migration_plan: int32 [4, 128, 1], P('span'), may hold values from 0 to 7; in each aligned block of 16 rows (0 to 15, 16 to 31, ..., all dimensions but the last counted through in order) at most 2 rows name the same one
- block_nodes: int32 [4, 128, 256], P('span'), may hold values from 0 to 8383, as said below
- corner_slot: int32 [4, 128, 4, 128], P('span'), may hold values from 0 to 255
Outputs:
- displacement_out: float32 [4, 5, 8192], P('span', None, 'grp')
- velocity_out: float32 [4, 5, 8192], P('span', None, 'grp')
- resident_plastic: float32 [4, 128, 3, 5, 128], P('span', 'grp')
- resident_hardening: float32 [4, 128, 5, 128], P('span', 'grp')
Inputs may be any that keep to these rules, and one draw needn't show every extreme that they name: `migration_plan`: of the 16 blocks that start on one device (aligned blocks of 16 entries), no more than 2 name the same device. `cost_map`: newton turns of a block. `block_nodes`: block b of a span group (0 to 127) lists 256 distinct nodes from b * (64) on.
All inputs are finite; a program needn't handle non-finite values.
Results may differ from a plain program's by a relative error of at most 0.0003.
Values sent between devices are 32-bit elements; how exact they have to be, the bound alone decides.
A program may use at most 64 MiB of HBM per device.

v0:
```python
import jax
import jax.numpy as jnp
from jax import lax
from jax.sharding import PartitionSpec as P

NEWTON = 4
STEPS = 4


POISSON = 0.3
YIELD = 0.1
SATURATE = 0.1
RATE = 20.0
STEP_TIME = 0.25
HIGHEST = lax.Precision.HIGHEST


def from_behind(shard, axis, by):
    size = lax.axis_size(axis)
    pairs = [(i, i + by) for i in range(size) if 0 <= i + by < size]
    return lax.ppermute(shard, axis, pairs)


def element_update(corner_disp, inverse_size, modulus, plastic, harden, costs):
    corner_a = corner_disp[:, :, 0]
    corner_b = corner_disp[:, :, 1]
    corner_c = corner_disp[:, :, 2]
    corner_d = corner_disp[:, :, 3]
    inverse = inverse_size[:, None, :]
    deriv_x = 0.5 * inverse * (corner_b + corner_c - corner_a - corner_d)
    deriv_y = 0.5 * inverse * (corner_c + corner_d - corner_a - corner_b)
    centre = 0.25 * (corner_a + corner_b + corner_c + corner_d)
    membrane = jnp.stack([deriv_x[:, 0], deriv_y[:, 1], deriv_y[:, 0] + deriv_x[:, 1]], 1)
    bending = jnp.stack([deriv_x[:, 3], deriv_y[:, 4], deriv_y[:, 3] + deriv_x[:, 4]], 1)
    transverse = jnp.stack([deriv_x[:, 2] + centre[:, 3], deriv_y[:, 2] + centre[:, 4]], 1)
    heights = jnp.array([-0.5, -0.25, 0.0, 0.25, 0.5], jnp.float32)
    through = jnp.array([1.0, 4.0, 2.0, 4.0, 1.0], jnp.float32) / 12.0
    strains = membrane[:, :, None, :] + heights[None, None, :, None] * bending[:, :, None, :]
    elastic = strains - plastic
    stiffness = modulus / (1.0 - POISSON * POISSON)
    trial_stress = jnp.stack(
        [
            stiffness * (elastic[:, 0] + POISSON * elastic[:, 1]),
            stiffness * (POISSON * elastic[:, 0] + elastic[:, 1]),
            stiffness * 0.5 * (1.0 - POISSON) * elastic[:, 2],
        ],
        1,
    )
    equivalent = jnp.sqrt(
        (trial_stress[:, 0] - 0.5 * trial_stress[:, 1]) ** 2
        + 0.75 * trial_stress[:, 1] ** 2
        + 3.0 * trial_stress[:, 2] ** 2
    )
    shear_three = 1.5 * modulus / (1.0 + POISSON)
    initial_yield = YIELD + SATURATE * (1.0 - jnp.exp(-RATE * harden))
    step_size = jnp.zeros_like(equivalent)
    for newton_turn in range(NEWTON):
        hardness = harden + step_size
        decay_term = jnp.exp(-RATE * hardness)
        mismatch = equivalent - shear_three * step_size - YIELD - SATURATE * (1.0 - decay_term)
        tangent = shear_three + SATURATE * RATE * decay_term
        active = (newton_turn < costs)[:, None, None]
        step_size = jnp.where(active, step_size + mismatch / tangent, step_size)
    step_size = jnp.where(equivalent > initial_yield, step_size, 0.0)
    shrink = 1.0 - shear_three * step_size / jnp.maximum(equivalent, YIELD)
    stresses = shrink[:, None] * trial_stress
    plastic_new = plastic + (1.0 - shrink)[:, None] * elastic
    harden_new = harden + step_size
    membrane_force = jnp.sum(through[None, None, :, None] * stresses, axis=2)
    moments = jnp.sum((through * heights)[None, None, :, None] * stresses, axis=2)
    shear_modulus = (
        5.0 / 6.0 * jnp.sum(through[None, :, None] * modulus, axis=1) / (2.0 * (1.0 + POISSON))
    )
    shear_force = shear_modulus[:, None, :] * transverse
    weight_x = jnp.array([-0.5, 0.5, 0.5, -0.5], jnp.float32)[None, :, None]
    weight_y = jnp.array([-0.5, -0.5, 0.5, 0.5], jnp.float32)[None, :, None]
    force_u = inverse * (weight_x * membrane_force[:, 0:1] + weight_y * membrane_force[:, 2:3])
    force_v = inverse * (weight_y * membrane_force[:, 1:2] + weight_x * membrane_force[:, 2:3])
    force_w = inverse * (weight_x * shear_force[:, 0:1] + weight_y * shear_force[:, 1:2])
    force_a = (
        inverse * (weight_x * moments[:, 0:1] + weight_y * moments[:, 2:3])
        + 0.25 * shear_force[:, 0:1]
    )
    force_b = (
        inverse * (weight_y * moments[:, 1:2] + weight_x * moments[:, 2:3])
        + 0.25 * shear_force[:, 1:2]
    )
    forces = jnp.stack([force_u, force_v, force_w, force_a, force_b], 1)
    return (forces, plastic_new, harden_new)


def block_tables(nodes, slots, first_nodes, width):
    count = nodes.shape[0]
    corner_nodes = jnp.take_along_axis(nodes, slots.reshape(count, -1), axis=1)
    offsets = corner_nodes - first_nodes[:, None]
    return (jnp.arange(width, dtype=jnp.int32)[None, :, None] == offsets[:, None, :]).astype(
        jnp.float32
    )


def element_forces(windows, tables, state, costs):
    plastic, harden, modulus, inverse = state
    count = tables.shape[0]
    elements = tables.shape[2] // 4
    corner_disp = jnp.einsum("cbw,bwk->cbk", windows, tables, precision=HIGHEST)
    corner_disp = jnp.transpose(corner_disp.reshape(5, count, 4, elements), (1, 0, 2, 3))
    forces, plastic, harden = element_update(corner_disp, inverse, modulus, plastic, harden, costs)
    forces = jnp.transpose(forces, (1, 0, 2, 3)).reshape(5, count, 4 * elements)
    nodal = jnp.einsum("cbk,bwk->cbw", forces, tables, precision=HIGHEST)
    return (nodal, plastic, harden)


def home_windows(extended, stride, count, width):
    pieces = [
        extended[:, q * stride : q * stride + count * stride].reshape(5, count, stride)
        for q in range(width // stride)
    ]
    return jnp.concatenate(pieces, 2)


def home_fold(nodal, stride, count, width):
    total = jnp.zeros((5, count * stride + width), jnp.float32)
    for q in range(width // stride):
        piece = nodal[:, :, q * stride : (q + 1) * stride].reshape(5, count * stride)
        total = total.at[:, q * stride : q * stride + count * stride].add(piece)
    return total


def integrate(disp_now, vel_now, internal, load_now, mass_now, pinned):
    accel = (load_now - internal) / mass_now[None, :]
    vel_now = jnp.where(pinned, 0.0, vel_now + STEP_TIME * accel)
    return (disp_now + STEP_TIME * vel_now, vel_now)


def pack(pick, values):
    return jnp.einsum("sb,b...->s...", pick, values, precision=HIGHEST)


def on_device(
    displacement,
    velocity,
    nodal_load,
    nodal_mass,
    plastic_strain,
    hardening,
    ply_modulus,
    inverse_size,
    cost_map,
    migration_plan,
    block_nodes,
    corner_slot,
):
    group = lax.axis_size("grp")
    member = lax.axis_index("grp")
    station = lax.axis_index("span")
    own_nodes = displacement.shape[2]
    own_blocks = plastic_strain.shape[1]
    window = block_nodes.shape[2]
    stride = own_nodes // own_blocks
    capacity = max(1, (own_blocks + group - 1) // group)
    slots_all = group * capacity
    disp_now = displacement[0]
    vel_now = velocity[0]
    load_now = nodal_load[0]
    mass_now = nodal_mass[0]
    pinned = (station == 0) & (member == 0) & (jnp.arange(own_nodes)[None, :] < window)
    dests = migration_plan[0, :, 0].reshape(group, own_blocks)
    earlier = jnp.arange(own_blocks)[:, None] > jnp.arange(own_blocks)[None, :]
    same = dests[:, :, None] == dests[:, None, :]
    rank = jnp.sum(same & earlier[None], axis=2)
    target = dests * capacity + rank
    my_target = lax.dynamic_index_in_dim(target, member, 0, keepdims=False)
    pick = (jnp.arange(slots_all, dtype=jnp.int32)[:, None] == my_target[None, :]).astype(
        jnp.float32
    )
    first_block = member * own_blocks
    nodes_here = (
        lax.dynamic_slice_in_dim(block_nodes[0], first_block, own_blocks, 0) - member * own_nodes
    )
    slots_here = lax.dynamic_slice_in_dim(corner_slot[0], first_block, own_blocks, 0)
    costs = lax.dynamic_slice_in_dim(cost_map[0], first_block, own_blocks, 0)
    tables = block_tables(
        nodes_here, slots_here, jnp.arange(own_blocks, dtype=jnp.int32) * stride, window
    )
    plastic = plastic_strain[0]
    harden = hardening[0]
    modulus = ply_modulus[0]
    inverse = inverse_size[0]
    for time_step in range(STEPS):
        rim = from_behind(disp_now[:, :window], ("span", "grp"), -1)
        extended = jnp.concatenate([disp_now, rim], 1)
        windows = home_windows(extended, stride, own_blocks, window)
        nodal, plastic, harden = element_forces(
            windows, tables, (plastic, harden, modulus, inverse), costs
        )
        partial_value = home_fold(nodal, stride, own_blocks, window)
        carried = from_behind(partial_value[:, own_nodes:], ("span", "grp"), 1)
        internal = partial_value[:, :own_nodes].at[:, :window].add(carried)
        disp_now, vel_now = integrate(disp_now, vel_now, internal, load_now, mass_now, pinned)
    resident_plastic, resident_hardening = (
        lax.all_to_all(pack(pick, plastic), "grp", split_axis=0, concat_axis=0, tiled=True),
        lax.all_to_all(pack(pick, harden), "grp", split_axis=0, concat_axis=0, tiled=True),
    )
    return (disp_now[None], vel_now[None], resident_plastic[None], resident_hardening[None])


def solution(mesh):
    return jax.shard_map(
        on_device,
        mesh=mesh,
        in_specs=(
            P("span", None, "grp"),
            P("span", None, "grp"),
            P("span", None, "grp"),
            P("span", "grp"),
            P("span", "grp", None, None, None),
            P("span", "grp", None, None),
            P("span", "grp", None, None),
            P("span", "grp", None),
            P("span", None),
            P("span", None, None),
            P("span", None, None),
            P("span", None, None, None),
        ),
        out_specs=(
            P("span", None, "grp"),
            P("span", None, "grp"),
            P("span", "grp", None, None, None),
            P("span", "grp", None, None),
        ),
        check_vma=False,
    )
```

profile of v0, /device:TPU:0, one launch (start us, length us, event | category | flops | bytes accessed | tf_op | source)
XLA Modules:
  0.0 183.5 jit_solution(1367604053983892425)
XLA Ops:
  0.6 0.8 copy.351
  1.4 1.3 collective-permute-start
  2.7 0.7 broadcast_multiply_fusion.1
  3.5 0.9 fusion.124
  4.3 0.7 compare_bitcast_fusion.3
  5.1 0.7 subtract_bitcast_fusion.4
  5.8 65.0 %gather_fusion = s32[8192]{0:T(1024)S(1)} fusion(s32[16,256]{1,0:T(8,128)S(1)} %subtract_bitcast_fusion.4, s32[8192]{0:T(1024)S(1)} %bitcast.966), kind=kCustom, calls=%fused_computation | custom fusion | bytes 131072 | tf_op jit(solution)/shard_map/jit(take_along_axis)/gather | solution.py:94
  71.1 0.6 compare_reduce_fusion.4
  71.8 0.6 compare_reduce_fusion.3
  72.4 0.6 compare_reduce_fusion.2
  73.0 0.6 compare_reduce_fusion.1
  74.1 2.7 %fusion.16 = f32[5,16,512]{2,0,1:T(8,128)S(1)} fusion(s32[16,512]{1,0:T(8,128)S(1)} %select_subtract_fusion, f32[5,16,64]{2,0,1:T(8,128)S(1)} %copy.198, f32[5,16,64]{2,0,1:T(8,128)S(1)} %copy.197, f32[5,16,64]{2,0,1:T(8,128)S(1)} %copy.196, f32[5,16,64]{2,0,1:T(8,128)S(1)} %copy.195), kind=kOutput, calls=%fused_computation.18 | convolution fusion | flops 127987712 | bytes 278528 | tf_op jit(solution)/shard_map/cbw,bwk->cbk/dot_general | solution.py:105
  77.2 0.8 copy-done.2
  79.6 3.8 %fusion.20 = f32[5,16,256]{2,0,1:T(8,128)S(1)} fusion(s32[16,512]{1,0:T(8,128)S(1)} %select_subtract_fusion, f32[5,16,512]{2,1,0:T(8,128)S(1)} %reshape.1161), kind=kOutput, calls=%fused_computation.22 | convolution fusion | flops 127926272 | bytes 278528 | tf_op jit(solution)/shard_map/cbk,bwk->cbw/dot_general | solution.py:109
  83.4 0.8 fusion.511
  84.6 0.7 add_select_fusion.35
  85.8 0.7 fusion.426
  86.5 0.7 add_select_fusion.33
  87.7 3.0 %collective-permute-start.1 = (f32[5,256]{1,0:T(8,128)S(1)}, f32[5,256]{1,0:T(8,128)S(1)}, u32[]{:S(2)}, u32[]{:S(2)}) collective-permute-start(f32[5,256]{1,0:T(8,128)S(1)} %slice.1046), channel_id=1, source_target_pairs={{0,1},{1,2},{2,3},{3,4},{4,5},{5,6},{6,7},{7,8},{8,9},{9,10},{10,1... | collective-permute-start | bytes 15368 | tf_op jit(solution)/shard_map/ppermute | solution.py:21
  90.7 0.7 compare_reduce_fusion
  91.5 0.6 fusion.468
  92.2 1.5 collective-permute-start.2
  93.8 3.5 %collective-permute-done.2 = f32[5,256]{1,0:T(8,128)S(1)} collective-permute-done((f32[5,256]{1,0:T(8,128)S(1)}, f32[5,256]{1,0:T(8,128)S(1)}, u32[]{:S(2)}, u32[]{:S(2)}) %collective-permute-start.2) | collective-permute-done | bytes 5152 | tf_op jit(solution)/shard_map/ppermute | solution.py:21
  97.7 2.7 %fusion.17 = f32[5,16,512]{2,0,1:T(8,128)S(1)} fusion(s32[16,512]{1,0:T(8,128)S(1)} %select_subtract_fusion, f32[5,16,64]{2,0,1:T(8,128)S(1)} %copy.210, f32[5,16,64]{2,0,1:T(8,128)S(1)} %copy.209, f32[5,16,64]{2,0,1:T(8,128)S(1)} %copy.208, f32[5,16,64]{2,0,1:T(8,128)S(1)} %copy.207), kind=kOutput, calls=%fused_computation.19 | convolution fusion | flops 127987712 | bytes 278528 | tf_op jit(solution)/shard_map/cbw,bwk->cbk/dot_general | solution.py:105
  101.6 3.8 %fusion.21 = f32[5,16,256]{2,0,1:T(8,128)S(1)} fusion(s32[16,512]{1,0:T(8,128)S(1)} %select_subtract_fusion, f32[5,16,512]{2,1,0:T(8,128)S(1)} %reshape.1171), kind=kOutput, calls=%fused_computation.23 | convolution fusion | flops 127926272 | bytes 278528 | tf_op jit(solution)/shard_map/cbk,bwk->cbw/dot_general | solution.py:109
  105.4 0.8 fusion.510
  106.5 0.7 add_select_fusion.32
  107.8 0.7 fusion.427
  108.4 0.7 add_select_fusion.30
  109.7 4.9 %collective-permute-start.3 = (f32[5,256]{1,0:T(8,128)S(1)}, f32[5,256]{1,0:T(8,128)S(1)}, u32[]{:S(2)}, u32[]{:S(2)}) collective-permute-start(f32[5,256]{1,0:T(8,128)S(1)} %slice.1087), channel_id=1, source_target_pairs={{0,1},{1,2},{2,3},{3,4},{4,5},{5,6},{6,7},{7,8},{8,9},{9,10},{10,1... | collective-permute-start | bytes 15368 | tf_op jit(solution)/shard_map/ppermute | solution.py:21
  115.0 0.6 reduce.74
  115.7 0.6 fusion.469
  116.4 1.5 collective-permute-start.4
  118.3 1.2 collective-permute-done.4
  119.8 2.7 %fusion.18 = f32[5,16,512]{2,0,1:T(8,128)S(1)} fusion(s32[16,512]{1,0:T(8,128)S(1)} %select_subtract_fusion, f32[5,16,64]{2,0,1:T(8,128)S(1)} %copy.221, f32[5,16,64]{2,0,1:T(8,128)S(1)} %copy.220, f32[5,16,64]{2,0,1:T(8,128)S(1)} %copy.219, f32[5,16,64]{2,0,1:T(8,128)S(1)} %copy.218), kind=kOutput, calls=%fused_computation.20 | convolution fusion | flops 127987712 | bytes 278528 | tf_op jit(solution)/shard_map/cbw,bwk->cbk/dot_general | solution.py:105
  123.7 3.8 %fusion.22 = f32[5,16,256]{2,0,1:T(8,128)S(1)} fusion(s32[16,512]{1,0:T(8,128)S(1)} %select_subtract_fusion, f32[5,16,512]{2,1,0:T(8,128)S(1)} %reshape.1181), kind=kOutput, calls=%fused_computation.24 | convolution fusion | flops 127926272 | bytes 278528 | tf_op jit(solution)/shard_map/cbk,bwk->cbw/dot_general | solution.py:109
  127.6 0.8 fusion.509
  128.7 0.7 add_select_fusion.29
  129.9 0.7 fusion.428
  130.6 0.7 add_select_fusion.27
  131.8 5.4 %collective-permute-start.5 = (f32[5,256]{1,0:T(8,128)S(1)}, f32[5,256]{1,0:T(8,128)S(1)}, u32[]{:S(2)}, u32[]{:S(2)}) collective-permute-start(f32[5,256]{1,0:T(8,128)S(1)} %slice.1128), channel_id=1, source_target_pairs={{0,1},{1,2},{2,3},{3,4},{4,5},{5,6},{6,7},{7,8},{8,9},{9,10},{10,1... | collective-permute-start | bytes 15368 | tf_op jit(solution)/shard_map/ppermute | solution.py:21
  137.3 0.8 collective-permute-done.5
  138.1 0.6 fusion.470
  138.7 1.6 collective-permute-start.6
  140.4 1.4 collective-permute-done.6
  142.2 2.7 %fusion.19 = f32[5,16,512]{2,0,1:T(8,128)S(1)} fusion(s32[16,512]{1,0:T(8,128)S(1)} %select_subtract_fusion, f32[5,16,64]{2,0,1:T(8,128)S(1)} %copy.232, f32[5,16,64]{2,0,1:T(8,128)S(1)} %copy.231, f32[5,16,64]{2,0,1:T(8,128)S(1)} %copy.230, f32[5,16,64]{2,0,1:T(8,128)S(1)} %copy.229), kind=kOutput, calls=%fused_computation.21 | convolution fusion | flops 127987712 | bytes 278528 | tf_op jit(solution)/shard_map/cbw,bwk->cbk/dot_general | solution.py:105
  146.1 3.8 %fusion.23 = f32[5,16,256]{2,0,1:T(8,128)S(1)} fusion(s32[16,512]{1,0:T(8,128)S(1)} %select_subtract_fusion, f32[5,16,512]{2,1,0:T(8,128)S(1)} %reshape.1191), kind=kOutput, calls=%fused_computation.25 | convolution fusion | flops 127926272 | bytes 278528 | tf_op jit(solution)/shard_map/cbk,bwk->cbw/dot_general | solution.py:109
  149.9 0.8 fusion.508
  151.1 0.7 add_select_fusion.26
  152.3 0.7 fusion.429
  153.0 0.7 add_select_fusion.24
  154.2 0.9 fusion.75
  155.1 0.6 copy.241
  155.7 11.5 %all-to-all-start.1 = ((f32[16,5,128]{2,1,0:T(8,128)}), f32[16,5,128]{2,1,0:T(8,128)S(1)}, u32[]{:S(2)}, u32[]{:S(2)}) async-start(f32[16,5,128]{2,1,0:T(8,128)} %copy.241), calls=%async_computation.1 | async-start | bytes 131072 | tf_op jit(solution)/shard_map/all_to_all | solution.py:202
  167.2 2.4 %collective-permute-start.7 = (f32[5,256]{1,0:T(8,128)S(1)}, f32[5,256]{1,0:T(8,128)S(1)}, u32[]{:S(2)}, u32[]{:S(2)}) collective-permute-start(f32[5,256]{1,0:T(8,128)S(1)} %slice.1169), channel_id=1, source_target_pairs={{0,1},{1,2},{2,3},{3,4},{4,5},{5,6},{6,7},{7,8},{8,9},{9,10},{10,1... | collective-permute-start | bytes 15368 | tf_op jit(solution)/shard_map/ppermute | solution.py:21
  169.9 0.7 copy.240
  170.6 0.6 fusion.471
  171.2 1.0 all-to-all-done.1
  172.2 4.8 %all-to-all-start = ((f32[16,3,5,128]{3,1,2,0:T(4,128)}), f32[16,3,5,128]{3,1,2,0:T(4,128)S(1)}, u32[]{:S(2)}, u32[]{:S(2)}) async-start(f32[16,3,5,128]{3,1,2,0:T(4,128)} %copy.240), calls=%async_computation | async-start | bytes 327680 | tf_op jit(solution)/shard_map/all_to_all | solution.py:201
  177.0 0.6 copy.242
  177.6 0.6 copy.243
  178.3 0.6 copy.245
  178.9 4.0 %all-to-all-done = f32[16,3,5,128]{3,1,2,0:T(4,128)S(1)} async-done(((f32[16,3,5,128]{3,1,2,0:T(4,128)}), f32[16,3,5,128]{3,1,2,0:T(4,128)S(1)}, u32[]{:S(2)}, u32[]{:S(2)}) %all-to-all-start) | async-done | bytes 122912 | tf_op jit(solution)/shard_map/all_to_all | solution.py:201
  182.9 0.7 copy.244
  (224 shorter events, 13.9 us)
Async XLA Ops:
  0.6 4.4 %copy-start = (s32[1,128,4,128]{3,2,1,0:T(4,128)S(1)}, s32[1,128,4,128]{3,2,1,0:T(4,128)}, u32[]{:S(2)}) copy-start(s32[1,128,4,128]{3,2,1,0:T(4,128)} %param.79) | copy-start | bytes 786436
  1.4 72.2 %collective-permute-start = (f32[5,256]{1,0:T(8,128)S(1)}, f32[5,256]{1,0:T(8,128)S(1)}, u32[]{:S(2)}, u32[]{:S(2)}) collective-permute-start(f32[5,256]{1,0:T(8,128)S(1)} %slice.1006), channel_id=1, source_target_pairs={{1,0},{2,1},{3,2},{4,3},{5,4},{6,5},{7,6},{8,7},{9,8},{10,9},{11,1... | collective-permute-start | bytes 15368 | tf_op jit(solution)/shard_map/ppermute | solution.py:21
  5.8 65.1 %copy-start.8 = (f32[1,5,1024]{2,0,1:T(1,128)S(1)}, f32[1,5,1024]{2,0,1:T(1,128)}, u32[]{:S(2)}) copy-start(f32[1,5,1024]{2,0,1:T(1,128)} %param.68) | copy-start | bytes 61444
  77.1 0.9 copy-start.2
  77.1 0.9 copy-start.11
  77.1 1.0 copy-start.3
  77.2 1.0 copy-start.4
  78.1 0.7 copy-start.12
  78.1 0.7 copy-start.13
  78.3 0.7 copy-start.1
  78.3 0.7 copy-start.6
  78.3 0.7 copy-start.7
  84.5 7.6 %copy-start.5 = (f32[1,5,1024]{2,0,1:T(1,128)S(1)}, f32[1,5,1024]{2,0,1:T(1,128)}, u32[]{:S(2)}) copy-start(f32[1,5,1024]{2,0,1:T(1,128)} %param.70) | copy-start | bytes 61444
  84.5 7.6 %copy-start.9 = (f32[1,5,1024]{2,0,1:T(1,128)S(1)}, f32[1,5,1024]{2,0,1:T(1,128)}, u32[]{:S(2)}) copy-start(f32[1,5,1024]{2,0,1:T(1,128)} %param.69) | copy-start | bytes 61444
  84.5 7.6 %copy-start.10 = (f32[1,1024]{1,0:T(1,128)S(1)}, f32[1,1024]{1,0:T(1,128)}, u32[]{:S(2)}) copy-start(f32[1,1024]{1,0:T(1,128)} %param.71) | copy-start | bytes 12292
  87.7 3.8 %collective-permute-start.1 = (f32[5,256]{1,0:T(8,128)S(1)}, f32[5,256]{1,0:T(8,128)S(1)}, u32[]{:S(2)}, u32[]{:S(2)}) collective-permute-start(f32[5,256]{1,0:T(8,128)S(1)} %slice.1046), channel_id=1, source_target_pairs={{0,1},{1,2},{2,3},{3,4},{4,5},{5,6},{6,7},{7,8},{8,9},{9,10},{10,1... | collective-permute-start | bytes 15368 | tf_op jit(solution)/shard_map/ppermute | solution.py:21
  92.2 5.1 %collective-permute-start.2 = (f32[5,256]{1,0:T(8,128)S(1)}, f32[5,256]{1,0:T(8,128)S(1)}, u32[]{:S(2)}, u32[]{:S(2)}) collective-permute-start(f32[5,256]{1,0:T(8,128)S(1)} %slice.1047), channel_id=1, source_target_pairs={{1,0},{2,1},{3,2},{4,3},{5,4},{6,5},{7,6},{8,7},{9,8},{10,9},{11,1... | collective-permute-start | bytes 15368 | tf_op jit(solution)/shard_map/ppermute | solution.py:21
  106.5 8.5 %copy-start.14 = (s32[1,128,1]{1,2,0:T(1,128)S(1)}, s32[1,128,1]{1,2,0:T(1,128)}, u32[]{:S(2)}) copy-start(s32[1,128,1]{1,2,0:T(1,128)} %param.77) | copy-start | bytes 1540
  109.7 6.1 %collective-permute-start.3 = (f32[5,256]{1,0:T(8,128)S(1)}, f32[5,256]{1,0:T(8,128)S(1)}, u32[]{:S(2)}, u32[]{:S(2)}) collective-permute-start(f32[5,256]{1,0:T(8,128)S(1)} %slice.1087), channel_id=1, source_target_pairs={{0,1},{1,2},{2,3},{3,4},{4,5},{5,6},{6,7},{7,8},{8,9},{9,10},{10,1... | collective-permute-start | bytes 15368 | tf_op jit(solution)/shard_map/ppermute | solution.py:21
  116.4 3.1 %collective-permute-start.4 = (f32[5,256]{1,0:T(8,128)S(1)}, f32[5,256]{1,0:T(8,128)S(1)}, u32[]{:S(2)}, u32[]{:S(2)}) collective-permute-start(f32[5,256]{1,0:T(8,128)S(1)} %slice.1088), channel_id=1, source_target_pairs={{1,0},{2,1},{3,2},{4,3},{5,4},{6,5},{7,6},{8,7},{9,8},{10,9},{11,1... | collective-permute-start | bytes 15368 | tf_op jit(solution)/shard_map/ppermute | solution.py:21
  131.8 6.3 %collective-permute-start.5 = (f32[5,256]{1,0:T(8,128)S(1)}, f32[5,256]{1,0:T(8,128)S(1)}, u32[]{:S(2)}, u32[]{:S(2)}) collective-permute-start(f32[5,256]{1,0:T(8,128)S(1)} %slice.1128), channel_id=1, source_target_pairs={{0,1},{1,2},{2,3},{3,4},{4,5},{5,6},{6,7},{7,8},{8,9},{9,10},{10,1... | collective-permute-start | bytes 15368 | tf_op jit(solution)/shard_map/ppermute | solution.py:21
  138.7 3.1 %collective-permute-start.6 = (f32[5,256]{1,0:T(8,128)S(1)}, f32[5,256]{1,0:T(8,128)S(1)}, u32[]{:S(2)}, u32[]{:S(2)}) collective-permute-start(f32[5,256]{1,0:T(8,128)S(1)} %slice.1129), channel_id=1, source_target_pairs={{1,0},{2,1},{3,2},{4,3},{5,4},{6,5},{7,6},{8,7},{9,8},{10,9},{11,1... | collective-permute-start | bytes 15368 | tf_op jit(solution)/shard_map/ppermute | solution.py:21
  155.7 16.5 %all-to-all-start.1 = ((f32[16,5,128]{2,1,0:T(8,128)}), f32[16,5,128]{2,1,0:T(8,128)S(1)}, u32[]{:S(2)}, u32[]{:S(2)}) async-start(f32[16,5,128]{2,1,0:T(8,128)} %copy.241), calls=%async_computation.1 | async-start | bytes 131072 | tf_op jit(solution)/shard_map/all_to_all | solution.py:202
  167.2 3.4 %collective-permute-start.7 = (f32[5,256]{1,0:T(8,128)S(1)}, f32[5,256]{1,0:T(8,128)S(1)}, u32[]{:S(2)}, u32[]{:S(2)}) collective-permute-start(f32[5,256]{1,0:T(8,128)S(1)} %slice.1169), channel_id=1, source_target_pairs={{0,1},{1,2},{2,3},{3,4},{4,5},{5,6},{6,7},{7,8},{8,9},{9,10},{10,1... | collective-permute-start | bytes 15368 | tf_op jit(solution)/shard_map/ppermute | solution.py:21
  172.2 10.7 %all-to-all-start = ((f32[16,3,5,128]{3,1,2,0:T(4,128)}), f32[16,3,5,128]{3,1,2,0:T(4,128)S(1)}, u32[]{:S(2)}, u32[]{:S(2)}) async-start(f32[16,3,5,128]{3,1,2,0:T(4,128)} %copy.240), calls=%async_computation | async-start | bytes 327680 | tf_op jit(solution)/shard_map/all_to_all | solution.py:201
where the time goes:
time: 184 us
  local copies, waits for them, and re-layouts  79.5 us (43%)
  starting transfers between devices  37.8 us (21%)
  matrix products  27.3 us (15%)
  other arithmetic  25.2 us (14%)
  waiting for transfers between devices  11.9 us (6%)
    gather x2, local copies, waits for them, and re-layouts, block_tables(): corner_nodes = jnp.take_along_axis(nodes, slots.reshape(count, -1), axis=1)  65 us
    ppermute x8, starting transfers between devices, from_behind(): return lax.ppermute(shard, axis, pairs)  21.6 us
    dot_general x4, matrix products, element_forces(): nodal = jnp.einsum('cbk,bwk->cbw', forces, tables, precision=HIGHEST)  15.3 us
    all_to_all x1, starting transfers between devices, on_device(): lax.all_to_all(pack(pick, harden), 'grp', split_axis=0, concat_axis=0, ti...  11.5 us
    dot_general x4, matrix products, element_forces(): corner_disp = jnp.einsum('cbw,bwk->cbk', windows, tables, precision=HIGHEST)  10.9 us
    another operation x13, other arithmetic  9.02 us
    ppermute x8, waiting for transfers between devices, from_behind(): return lax.ppermute(shard, axis, pairs)  6.96 us
    unnamed x37, local copies, waits for them, and re-layouts  5.27 us
  transfers between devices with their start and end apart: 10, of which 7 were waited for; matrix products, arithmetic and copies ran while one was open for 42% of the time, Pallas kernels for 0%

commit v1 on v0

v1 whole, which is shorter than its diff:
```python
import functools

import jax
import jax.numpy as jnp
from jax import lax
from jax.experimental import pallas as pl
from jax.experimental.pallas import tpu as pltpu
from jax.sharding import PartitionSpec as P

NEWTON = 4
STEPS = 4

POISSON = 0.3
YIELD = 0.1
SATURATE = 0.1
RATE = 20.0
STEP_TIME = 0.25
HEIGHTS = (-0.5, -0.25, 0.0, 0.25, 0.5)
THROUGH = (1.0 / 12.0, 4.0 / 12.0, 2.0 / 12.0, 4.0 / 12.0, 1.0 / 12.0)
WEIGHT_X = (-0.5, 0.5, 0.5, -0.5)
WEIGHT_Y = (-0.5, -0.5, 0.5, 0.5)
MESH = pl.DeviceIdType.MESH
LANES = 128
ROWS = 8
FREE = 5


def pad_rows(x):
    return jnp.concatenate([x, jnp.zeros((ROWS - x.shape[0], x.shape[1]), x.dtype)], 0)


def lane_take(x, index):
    return jnp.take_along_axis(x, index, axis=1, mode="promise_in_bounds")


def split_rows(ref_rows, reach):
    return (
        jnp.concatenate([ref_rows[:reach], ref_rows[-reach:]], 0),
        ref_rows[reach:-reach],
    )


def join_rows(outer, inner, reach):
    return jnp.concatenate([outer[:reach], inner, outer[reach:]], 0)


def kernel(
    sizes,
    disp_hbm, vel_hbm, load_hbm, mass_hbm, plastic_hbm, harden_hbm, modulus_hbm, inverse_hbm,
    cost_hbm, plan_hbm, nodes_hbm, slots_hbm,
    disp_out, vel_out, plastic_out, harden_out,
    disp_in, vel_in, load_in, mass_in, plastic_in, harden_in, modulus_in, inverse_in,
    cost_in, plan_in, nodes_in, slots_in,
    rim_out, rim_in, ahead_out, ahead_in, back_out, back_in,
    disp, vel, load, mass, lane_at, half_at, tables, windows, spread, partial,
    plastic, harden, modulus, inverse, costs, pack_out, pack_in,
    in_sems, rim_sems, ahead_sems, back_sems, move_sems,
):
    spans, group, own_nodes, own_blocks, window, stride, reach, capacity = sizes
    points = harden_in.shape[0]
    corners = slots_in.shape[1]
    own_chunks = own_nodes // LANES
    rim_chunks = window // LANES
    chunks = own_chunks + rim_chunks
    station = lax.axis_index("span")
    member = lax.axis_index("grp")
    has_next = jnp.logical_not((station == spans - 1) & (member == group - 1))
    has_prev = jnp.logical_not((station == 0) & (member == 0))
    next_id = (lax.rem(station + (member + 1) // group, spans), lax.rem(member + 1, group))
    prev_id = (
        lax.rem(station + spans - 1 + (member + group - 1) // group, spans),
        lax.rem(member + group - 1, group),
    )
    outer_up = (member == group - 1) & has_next
    outer_down = (member == 0) & has_prev

    barrier = pltpu.get_barrier_semaphore()
    for j in range(1, group):
        pl.semaphore_signal(
            barrier, inc=1, device_id=(station, lax.rem(member + j, group)), device_id_type=MESH
        )

    @pl.when(outer_up)
    def _():
        pl.semaphore_signal(barrier, inc=1, device_id=next_id, device_id_type=MESH)

    @pl.when(outer_down)
    def _():
        pl.semaphore_signal(barrier, inc=1, device_id=prev_id, device_id_type=MESH)

    first = pl.multiple_of(member * own_blocks, own_blocks)
    pairs = [
        (disp_hbm, disp_in),
        (vel_hbm, vel_in),
        (load_hbm, load_in),
        (mass_hbm, mass_in),
        (plastic_hbm, plastic_in),
        (harden_hbm, harden_in),
        (modulus_hbm, modulus_in),
        (inverse_hbm.at[0], inverse_in),
        (cost_hbm, cost_in),
        (plan_hbm, plan_in),
        (nodes_hbm.at[0, pl.ds(first, own_blocks)], nodes_in),
        (slots_hbm.at[0, pl.ds(first, own_blocks)], slots_in),
    ]
    loads = [pltpu.make_async_copy(a, b, in_sems.at[i]) for i, (a, b) in enumerate(pairs)]
    for copy in loads:
        copy.start()
    for copy in loads[:4]:
        copy.wait()
    def cut(q):
        return slice(q * LANES, (q + 1) * LANES)

    def chunk(ref, q):
        return pad_rows(ref[pl.ds(q, FREE, stride=own_chunks), :])

    def mass_chunk(q):
        return jnp.broadcast_to(mass_in[q : q + 1, :], (ROWS, LANES))

    for q in range(rim_chunks):
        for i, ref in enumerate((disp_in, vel_in, load_in)):
            rim_out[i, :, cut(q)] = chunk(ref, q)
        rim_out[3, :, cut(q)] = mass_chunk(q)

    greeted = group - 1 + jnp.where(outer_up, 1, 0) + jnp.where(outer_down, 1, 0)
    pl.semaphore_wait(barrier, greeted)

    def rim_copy():
        return pltpu.make_async_remote_copy(
            src_ref=rim_out, dst_ref=rim_in, send_sem=rim_sems.at[0], recv_sem=rim_sems.at[1],
            device_id=prev_id, device_id_type=MESH,
        )

    def ahead_copy(step):
        return pltpu.make_async_remote_copy(
            src_ref=ahead_out.at[step], dst_ref=ahead_in.at[step],
            send_sem=ahead_sems.at[0, step], recv_sem=ahead_sems.at[1, step],
            device_id=next_id, device_id_type=MESH,
        )

    def back_copy(step):
        return pltpu.make_async_remote_copy(
            src_ref=back_out.at[step], dst_ref=back_in.at[step],
            send_sem=back_sems.at[0, step], recv_sem=back_sems.at[1, step],
            device_id=prev_id, device_id_type=MESH,
        )

    @pl.when(has_prev)
    def _():
        rim_copy().start()

    for q in range(own_chunks):
        for source, target in ((disp_in, disp), (vel_in, vel), (load_in, load)):
            target[:, cut(q)] = chunk(source, q)
        mass[:, cut(q)] = STEP_TIME / mass_chunk(q)
    spread[...] = jnp.zeros_like(spread)
    for copy in loads[8:]:
        copy.wait()
    node_row = lax.broadcasted_iota(jnp.int32, (own_blocks, 1), 0)
    local = nodes_in[...] - (first + node_row) * stride
    halves = window // LANES
    local_groups = split_rows(local, reach)
    for g in range(2):
        for k in range(corners):
            slot = split_rows(slots_in[:, k, :], reach)[g]
            low = slot & (LANES - 1)
            node = lane_take(local_groups[g][:, :LANES], low)
            for h in range(1, halves):
                part = lane_take(local_groups[g][:, h * LANES : (h + 1) * LANES], low)
                node = jnp.where(slot // LANES == h, part, node)
            lane_at[k, g * ROWS : (g + 1) * ROWS, :] = node & (LANES - 1)
            half_at[k, g * ROWS : (g + 1) * ROWS, :] = node // LANES
    lane_row = lax.broadcasted_iota(jnp.int32, (LANES, LANES), 0)

    def build(pos, carry):
        for k in range(corners):
            row = lane_at[k, pl.ds(pos, 1), :]
            hit = jnp.where(lane_row == row, 1.0, 0.0).astype(jnp.bfloat16)
            tables[pos, :, k * LANES : (k + 1) * LANES] = hit
        return carry

    lax.fori_loop(0, own_blocks, build, 0)

    width = cost_in.shape[1]
    at_block = lax.broadcasted_iota(jnp.int32, (own_blocks, width), 1)
    mine = at_block == first + lax.broadcasted_iota(jnp.int32, (own_blocks, width), 0)
    cost_column = jnp.sum(jnp.where(mine, cost_in[...], 0), axis=1, keepdims=True)
    cost_groups = split_rows(cost_column, reach)
    for g in range(2):
        costs[g] = jnp.broadcast_to(cost_groups[g], (ROWS, LANES))
    for copy in loads[4:8]:
        copy.wait()
    inverse_groups = split_rows(inverse_in[...], reach)
    for g in range(2):
        inverse[g] = inverse_groups[g]
    for p in range(points):
        for source, target in ((harden_in, harden), (modulus_in, modulus)):
            parts = split_rows(source[p], reach)
            for g in range(2):
                target[g, p] = parts[g]
        for c in range(3):
            parts = split_rows(plastic_in[c, p], reach)
            for g in range(2):
                plastic[g, c * points + p] = parts[g]

    @pl.when(has_prev)
    def _():
        rim_copy().wait_send()

    @pl.when(has_next)
    def _():
        rim_copy().wait_recv()

    rim = pl.ds(own_nodes, window)
    disp[:, rim] = jnp.where(has_next, rim_in[0], 0.0)
    vel[:, rim] = jnp.where(has_next, rim_in[1], 0.0)
    load[:, rim] = jnp.where(has_next, rim_in[2], 0.0)
    mass[:, rim] = jnp.where(has_next, STEP_TIME / rim_in[3], 0.0)

    order = list(range(reach)) + list(range(own_blocks - reach, own_blocks))
    order += list(range(reach, own_blocks - reach))
    phases = LANES // stride
    lane = lax.broadcasted_iota(jnp.int32, (ROWS, LANES), 1)

    def place_windows():
        shifted = {}
        for r in range(phases):
            for q in range(chunks - (1 if r else 0)):
                value = disp[:, cut(q)]
                if r:
                    left = LANES - r * stride
                    value = jnp.where(
                        lane < left,
                        pltpu.roll(value, left, 1),
                        pltpu.roll(disp[:, cut(q + 1)], left, 1),
                    )
                shifted[r, q] = value
        for pos, block in enumerate(order):
            for h in range(halves):
                value = shifted[block % phases, block // phases + h]
                windows[h, pos * ROWS : (pos + 1) * ROWS, :] = value

    def elements(g):
        lanes_of = [lane_at[k, g * ROWS : (g + 1) * ROWS, :] for k in range(corners)]
        halves_of = [half_at[k, g * ROWS : (g + 1) * ROWS, :] for k in range(corners)]
        corner = []
        for c in range(FREE):
            rows = [windows[h, pl.ds(g * ROWS * ROWS + c, ROWS, stride=ROWS), :] for h in range(halves)]
            values = []
            for k in range(corners):
                value = lane_take(rows[0], lanes_of[k])
                for h in range(1, halves):
                    value = jnp.where(halves_of[k] == h, lane_take(rows[h], lanes_of[k]), value)
                values.append(value)
            corner.append(values)
        z = inverse[g]
        half_z = 0.5 * z
        x = [half_z * (u[1] + u[2] - u[0] - u[3]) for u in corner]
        y = [half_z * (u[2] + u[3] - u[0] - u[1]) for u in corner]
        centre = [0.25 * (u[0] + u[1] + u[2] + u[3]) for u in corner[3:]]
        membrane = (x[0], y[1], y[0] + x[1])
        bending = (x[3], y[4], y[3] + x[4])
        transverse = (x[2] + centre[0], y[2] + centre[1])
        cost = costs[g]
        force = [jnp.zeros_like(z) for _ in range(3)]
        moment = [jnp.zeros_like(z) for _ in range(3)]
        stiff_sum = jnp.zeros_like(z)
        for p in range(points):
            young = modulus[g, p]
            old = harden[g, p]
            e = [membrane[c] + HEIGHTS[p] * bending[c] - plastic[g, c * points + p] for c in range(3)]
            stiff = young * (1.0 / (1.0 - POISSON * POISSON))
            trial = (
                stiff * (e[0] + POISSON * e[1]),
                stiff * (POISSON * e[0] + e[1]),
                stiff * (0.5 * (1.0 - POISSON)) * e[2],
            )
            first_part = trial[0] - 0.5 * trial[1]
            equal = jnp.sqrt(
                first_part * first_part + 0.75 * trial[1] * trial[1] + 3.0 * trial[2] * trial[2]
            )
            three = young * (1.5 / (1.0 + POISSON))
            decay = jnp.exp(-RATE * old)
            gap = equal - (YIELD + SATURATE)
            beyond = gap + SATURATE * decay
            change = beyond / (three + (SATURATE * RATE) * decay)
            yields = beyond > 0.0
            for turn in range(1, NEWTON):
                decay = jnp.exp(-RATE * (old + change))
                miss = gap - three * change + SATURATE * decay
                moved = change + miss / (three + (SATURATE * RATE) * decay)
                change = jnp.where(cost > turn, moved, change)
            change = jnp.where(yields & (cost > 0), change, 0.0)
            drop = three * change / jnp.maximum(equal, YIELD)
            keep = 1.0 - drop
            harden[g, p] = old + change
            for c in range(3):
                plastic[g, c * points + p] += drop * e[c]
                stress = keep * trial[c]
                force[c] = force[c] + THROUGH[p] * stress
                if HEIGHTS[p]:
                    moment[c] = moment[c] + (THROUGH[p] * HEIGHTS[p]) * stress
            stiff_sum = stiff_sum + THROUGH[p] * young
        shear = stiff_sum * (5.0 / 6.0 / (2.0 * (1.0 + POISSON)))
        q = (shear * transverse[0], shear * transverse[1])
        nx, ny, nxy = (z * v for v in force)
        mx, my, mxy = (z * v for v in moment)
        qx, qy = z * q[0], z * q[1]
        for k in range(corners):
            a, b = WEIGHT_X[k], WEIGHT_Y[k]
            values = (
                a * nx + b * nxy,
                b * ny + a * nxy,
                a * qx + b * qy,
                a * mx + b * mxy + 0.25 * q[0],
                b * my + a * mxy + 0.25 * q[1],
            )
            for c in range(FREE):
                for h in range(halves):
                    start = g * ROWS * halves * ROWS + h * ROWS + c
                    spread[k, pl.ds(start, ROWS, stride=halves * ROWS), :] = jnp.where(
                        halves_of[k] == h, values[c], 0.0
                    )

    def assemble(g):
        total = {}
        tall = halves * ROWS
        for pos in range(g * ROWS, (g + 1) * ROWS):
            block = order[pos]
            rows = jnp.concatenate(
                [spread[k, pos * tall : (pos + 1) * tall, :] for k in range(corners)], 1
            )
            high = rows.astype(jnp.bfloat16)
            low = (rows - high.astype(jnp.float32)).astype(jnp.bfloat16)
            out = lax.dot_general(
                jnp.concatenate([high, low], 0), tables[pos], (((1,), (1,)), ((), ())),
                preferred_element_type=jnp.float32,
            )
            out = out[:tall] + out[tall:]
            for h in range(halves):
                key = (block % phases, block // phases + h)
                piece = out[h * ROWS : (h + 1) * ROWS]
                total[key] = total[key] + piece if key in total else piece
        result = {}
        for (r, q), value in total.items():
            if r == 0:
                parts = ((q, value),)
            else:
                left = LANES - r * stride
                turned = pltpu.roll(value, r * stride, 1)
                parts = (
                    (q, jnp.where(lane >= r * stride, turned, 0.0)),
                    (q + 1, jnp.where(lane >= r * stride, 0.0, turned)),
                )
            for at, piece in parts:
                result[at] = result[at] + piece if at in result else piece
        return result

    pinned = (station == 0) & (member == 0)

    def forces(step, last):
        place_windows()
        elements(0)
        sums = assemble(0)
        for i in range(rim_chunks):
            ahead_out[step, :, cut(i)] = sums[own_chunks + i]
            if not last:
                back_out[step, :, cut(i)] = sums[i]

        @pl.when(has_next)
        def _():
            ahead_copy(step).start()

        if not last:
            @pl.when(has_prev)
            def _():
                back_copy(step).start()

        for q in range(chunks):
            partial[:, cut(q)] = sums.get(q, jnp.zeros((ROWS, LANES), jnp.float32))
        elements(1)

    def inner_sums():
        for q, value in assemble(1).items():
            partial[:, cut(q)] += value

    def finish(step, last):
        @pl.when(has_next)
        def _():
            ahead_copy(step).wait_send()

        @pl.when(has_prev)
        def _():
            ahead_copy(step).wait_recv()

        if not last:
            @pl.when(has_prev)
            def _():
                back_copy(step).wait_send()

            @pl.when(has_next)
            def _():
                back_copy(step).wait_recv()

        for q in range(own_chunks if last else chunks):
            internal = partial[:, cut(q)]
            if q < rim_chunks:
                internal = internal + jnp.where(has_prev, ahead_in[step, :, cut(q)], 0.0)
            if q >= own_chunks:
                internal = internal + jnp.where(
                    has_next, back_in[step, :, cut(q - own_chunks)], 0.0
                )
            speed = vel[:, cut(q)] + (load[:, cut(q)] - internal) * mass[:, cut(q)]
            if q < rim_chunks:
                speed = jnp.where(pinned, 0.0, speed)
            place = disp[:, cut(q)] + STEP_TIME * speed
            if last:
                vel_out[pl.ds(q, FREE, stride=own_chunks), :] = speed[:FREE]
                disp_out[pl.ds(q, FREE, stride=own_chunks), :] = place[:FREE]
            else:
                vel[:, cut(q)] = speed
                disp[:, cut(q)] = place

    def one_step(step, carry):
        forces(step, False)
        inner_sums()
        finish(step, False)
        return carry

    lax.fori_loop(0, STEPS - 1, one_step, 0)
    last = STEPS - 1
    forces(last, True)

    plan_column = jnp.sum(jnp.where(mine, plan_in[...], 0), axis=1, keepdims=True)
    row_at = lax.broadcasted_iota(jnp.int32, (own_blocks, own_blocks), 0)
    column_at = lax.broadcasted_iota(jnp.int32, (own_blocks, own_blocks), 1)
    plan_row = jnp.sum(jnp.where(row_at == column_at, plan_column, 0), axis=0, keepdims=True)
    rank = jnp.sum(
        jnp.where((row_at < column_at) & (plan_column == plan_row), 1, 0), axis=0, keepdims=True
    )
    slots_all = group * capacity
    slot_at = lax.broadcasted_iota(jnp.int32, (slots_all, own_blocks), 0)
    pick = jnp.where(slot_at == rank * group + plan_row, 1.0, 0.0)
    pick = jnp.concatenate([pick, pick, pick], 1).astype(jnp.bfloat16)

    def packed(ref, index):
        state = join_rows(ref[0, index], ref[1, index], reach)
        a = state.astype(jnp.bfloat16)
        rest = state - a.astype(jnp.float32)
        b = rest.astype(jnp.bfloat16)
        c = (rest - b.astype(jnp.float32)).astype(jnp.bfloat16)
        return jnp.dot(pick, jnp.concatenate([a, b, c], 0), preferred_element_type=jnp.float32)

    kinds = plastic_in.shape[0]
    fields = (kinds + 1) * points
    tall = fields * capacity
    for f in range(fields):
        rows = packed(plastic, f) if f < kinds * points else packed(harden, f - kinds * points)
        for r in range(capacity):
            pack_out[pl.ds(f * capacity + r, group, stride=tall), :] = rows[r * group : (r + 1) * group]

    def block_of(index):
        return pl.ds(pl.multiple_of(index * tall, ROWS), tall)

    def move(j):
        to = lax.rem(member + j, group)
        return pltpu.make_async_remote_copy(
            src_ref=pack_out.at[block_of(to)], dst_ref=pack_in.at[block_of(member)],
            send_sem=move_sems.at[0, j], recv_sem=move_sems.at[1, j],
            device_id=(station, to), device_id_type=MESH,
        )

    stay = pltpu.make_async_copy(
        pack_out.at[block_of(member)], pack_in.at[block_of(member)], move_sems.at[0, 0]
    )
    for j in range(1, group):
        move(j).start()
    stay.start()
    inner_sums()
    finish(last, True)
    stay.wait()
    for j in range(1, group):
        move(j).wait_send()
        move(j).wait_recv()
    for f in range(fields):
        c, p = f // points, f % points
        target = plastic_out.at[c, p] if c < kinds else harden_out.at[p]
        for r in range(capacity):
            rows = pack_in[pl.ds(f * capacity + r, group, stride=tall), :]
            target[pl.ds(r, group, stride=capacity), :] = rows


def on_device(
    displacement, velocity, nodal_load, nodal_mass, plastic_strain, hardening, ply_modulus,
    inverse_size, cost_map, migration_plan, block_nodes, corner_slot,
):
    spans, group = lax.axis_size("span"), lax.axis_size("grp")
    own_nodes = displacement.shape[2]
    own_blocks, kinds, points, size = plastic_strain.shape[1:]
    window = block_nodes.shape[2]
    corners = corner_slot.shape[2]
    stride = own_nodes // own_blocks
    reach = window // stride
    capacity = max(1, (own_blocks + group - 1) // group)
    halves = window // LANES
    slots_all = group * capacity
    chunks = own_nodes + window
    f32, i32 = jnp.float32, jnp.int32
    sizes = (spans, group, own_nodes, own_blocks, window, stride, reach, capacity)
    vmem = pltpu.VMEM
    dma = pltpu.SemaphoreType.DMA
    every = pl.BlockSpec(memory_space=pltpu.MemorySpace.HBM)
    whole = pl.BlockSpec(memory_space=pltpu.VMEM)
    nodal = (displacement.shape[1] * own_nodes // LANES, LANES)
    masses = (own_nodes // LANES, LANES)
    scratch = [
        vmem(nodal, f32), vmem(nodal, f32), vmem(nodal, f32), vmem(masses, f32),
        vmem((kinds, points, own_blocks, size), f32), vmem((points, own_blocks, size), f32),
        vmem((points, own_blocks, size), f32), vmem(inverse_size.shape[1:], f32),
        vmem(cost_map.shape, i32), vmem(cost_map.shape, i32),
        vmem((own_blocks, window), i32), vmem((own_blocks, corners, size), i32),
        vmem((4, ROWS, window), f32), vmem((4, ROWS, window), f32),
        vmem((STEPS, ROWS, window), f32), vmem((STEPS, ROWS, window), f32),
        vmem((STEPS, ROWS, window), f32), vmem((STEPS, ROWS, window), f32),
        vmem((ROWS, chunks), f32), vmem((ROWS, chunks), f32),
        vmem((ROWS, chunks), f32), vmem((ROWS, chunks), f32),
        vmem((corners, own_blocks, size), i32), vmem((corners, own_blocks, size), i32),
        vmem((own_blocks, LANES, corners * size), jnp.bfloat16),
        vmem((halves, own_blocks * ROWS, LANES), f32),
        vmem((corners, own_blocks * halves * ROWS, size), f32),
        vmem((ROWS, chunks), f32),
        vmem((2, kinds * points, ROWS, size), f32), vmem((2, points, ROWS, size), f32),
        vmem((2, points, ROWS, size), f32), vmem((2, ROWS, size), f32),
        vmem((2, ROWS, size), i32),
        vmem((slots_all * (kinds + 1) * points, size), f32),
        vmem((slots_all * (kinds + 1) * points, size), f32),
        dma((12,)), dma((2,)), dma((2, STEPS)), dma((2, STEPS)), dma((2, group)),
    ]
    disp, vel, moved, hardened = pl.pallas_call(
        functools.partial(kernel, sizes),
        out_shape=(
            jax.ShapeDtypeStruct(nodal, f32),
            jax.ShapeDtypeStruct(nodal, f32),
            jax.ShapeDtypeStruct((kinds, points, slots_all, size), f32),
            jax.ShapeDtypeStruct((points, slots_all, size), f32),
        ),
        in_specs=[every] * 12,
        out_specs=(whole,) * 4,
        scratch_shapes=scratch,
        compiler_params=pltpu.CompilerParams(
            collective_id=0, has_side_effects=True, vmem_limit_bytes=63 * 1024 * 1024
        ),
    )(
        displacement.reshape(nodal), velocity.reshape(nodal), nodal_load.reshape(nodal),
        nodal_mass.reshape(masses), jnp.transpose(plastic_strain[0], (1, 2, 0, 3)),
        jnp.transpose(hardening[0], (1, 0, 2)), jnp.transpose(ply_modulus[0], (1, 0, 2)),
        inverse_size, cost_map, migration_plan.reshape(cost_map.shape), block_nodes, corner_slot,
    )
    return (
        disp.reshape(displacement.shape),
        vel.reshape(displacement.shape),
        jnp.transpose(moved, (2, 0, 1, 3))[None],
        jnp.transpose(hardened, (1, 0, 2))[None],
    )


def solution(mesh):
    return jax.shard_map(
        on_device,
        mesh=mesh,
        in_specs=(
            P("span", None, "grp"),
            P("span", None, "grp"),
            P("span", None, "grp"),
            P("span", "grp"),
            P("span", "grp", None, None, None),
            P("span", "grp", None, None),
            P("span", "grp", None, None),
            P("span", "grp", None),
            P("span", None),
            P("span", None, None),
            P("span", None, None),
            P("span", None, None, None),
        ),
        out_specs=(
            P("span", None, "grp"),
            P("span", None, "grp"),
            P("span", "grp", None, None, None),
            P("span", "grp", None, None),
        ),
        check_vma=False,
    )
```

time: 184 us -> 28.8 us (0.16)
  local copies, waits for them, and re-layouts: 79.5 us -> 4.14 us
  starting transfers between devices: 37.8 us -> 0 us
  matrix products: 27.3 us -> 0 us
  other arithmetic: 25.2 us -> 0 us
  Pallas kernels: 0 us -> 23.8 us
  waiting for transfers between devices: 11.9 us -> 0 us
    gather x2 -> x0, local copies, waits for them, and re-layouts: 65 us -> none  [block_tables(): corner_nodes = jnp.take_along_axis(nodes, slots.reshape(count, -1), axis=1)]
    dot_general x10 -> x0, matrix products: 27.3 us -> none  [the longest x4 15.3 us: element_forces(): nodal = jnp.einsum('cbk,bwk->cbw', forces, tables, precision=HIGHEST)]
    pallas_call x0 -> x1, Pallas kernels: none -> 23.8 us  [on_device(): pl.pallas_call(functools.partial(kernel, sizes), out_shape=(jax.ShapeDtyp...]
    ppermute x8 -> x0, starting transfers between devices: 21.6 us -> none  [from_behind(): return lax.ppermute(shard, axis, pairs)]
    all_to_all x2 -> x0, starting transfers between devices: 16.2 us -> none  [the longest x1 11.5 us: on_device(): lax.all_to_all(pack(pick, harden), 'grp', split_axis=0, concat_axis=0, ti...]
    another operation x24 -> x0, other arithmetic: 9.41 us -> none
    ppermute x8 -> x0, waiting for transfers between devices: 6.96 us -> none  [from_behind(): return lax.ppermute(shard, axis, pairs)]
    scatter-add x8 -> x0, other arithmetic: 5.08 us -> none  [the longest x4 2.63 us: home_fold(): total = total.at[:, q * stride:q * stride + count * stride].add(piece)]
  transfers between devices with their start and end apart: 10 -> 0, of which waited for: 7 -> 0; matrix products, arithmetic and copies ran while one was open for 42% -> 0% of each run, Pallas kernels for 0% -> 0%
where the time goes in v1:
time: 28.8 us; the launch traced here: 28.6 us
  Pallas kernels  23.8 us (83%)
  local copies, waits for them, and re-layouts  4.14 us (14%)
  between operations  0.65 us (2%)
    pallas_call x1, Pallas kernels, on_device(): pl.pallas_call(functools.partial(kernel, sizes), out_shape=(jax.ShapeDtyp...  23.8 us
    unnamed x8, local copies, waits for them, and re-layouts  4.14 us

profile of v1, /device:TPU:0, one launch (start us, length us, event | category | flops | bytes accessed | tf_op | source)
XLA Modules:
  0.0 28.6 jit_solution(1420467196117542257)
XLA Ops:
  0.6 23.8 %shard_map.147 = (f32[40,128]{1,0:T(8,128)}, f32[40,128]{1,0:T(8,128)}, f32[3,5,16,128]{3,2,1,0:T(8,128)}, f32[5,16,128]{2,1,0:T(8,128)}) custom-call(f32[40,128]{1,0:T(8,128)} %bitcast.29, f32[40,128]{1,0:T(8,128)} %bitcast.30, f32[40,128]{1,0:T(8,128)} %bitcast.31, f32[8,128]{1,0:T(8,128)} %bitcast.32, f32[3,5,16,128]{3,2,1,0:T(8,128)} %bitcast.22, ...), custom_call_target="tpu_custom_call" | custom-call | tf_op jit(solution)/shard_map/pallas_call | solution.py:539
  24.4 0.0 copy-start.1
  24.4 1.3 %copy.24 = f32[1,5,1024]{2,0,1:T(1,128)} copy(f32[1,5,1024]{2,0,1:T(1,128)} %bitcast.28) | data formatting | bytes 40960
  25.8 0.0 copy-done.1
  25.8 0.6 %copy.25 = f32[1,5,1024]{2,0,1:T(1,128)} copy(f32[1,5,1024]{2,0,1:T(1,128)S(1)} %bitcast.27) | data formatting | bytes 40960
  26.4 0.0 copy-start
  26.4 1.6 %copy.26 = f32[1,16,3,5,128]{4,1,3,2,0:T(8,128)} copy(f32[1,16,3,5,128]{4,1,3,2,0:T(8,128)} %bitcast.23) | data formatting | bytes 245760
  28.0 0.0 copy-done
  28.0 0.6 %copy.27 = f32[1,16,5,128]{3,1,2,0:T(8,128)} copy(f32[1,16,5,128]{3,1,2,0:T(8,128)S(1)} %bitcast.24) | data formatting | bytes 81920
Async XLA Ops:
  24.4 1.4 %copy-start.1 = (f32[40,128]{1,0:T(8,128)S(1)}, f32[40,128]{1,0:T(8,128)}, u32[]{:S(2)}) copy-start(f32[40,128]{1,0:T(8,128)} %get-tuple-element.9) | copy-start | bytes 61444
  26.4 1.6 %copy-start = (f32[5,16,128]{2,1,0:T(8,128)S(1)}, f32[5,16,128]{2,1,0:T(8,128)}, u32[]{:S(2)}) copy-start(f32[5,16,128]{2,1,0:T(8,128)} %get-tuple-element.11) | copy-start | bytes 122884

commit v2 on v1

--- a/solution.py
+++ b/solution.py
@@ -490,6 +490,16 @@
             target[pl.ds(r, group, stride=capacity), :] = rows
 
 
+def hand_over(disp, vel, moved, hardened, disp_out, vel_out, moved_out, hardened_out, sems):
+    pairs = [(disp, disp_out), (vel, vel_out), (hardened, hardened_out)]
+    pairs += [(moved.at[c], moved_out.at[c]) for c in range(moved.shape[0])]
+    copies = [pltpu.make_async_copy(a, b, sems.at[i]) for i, (a, b) in enumerate(pairs)]
+    for copy in copies[::-1]:
+        copy.start()
+    for copy in copies:
+        copy.wait()
+
+
 def on_device(
     displacement, velocity, nodal_load, nodal_mass, plastic_strain, hardening, ply_modulus,
     inverse_size, cost_map, migration_plan, block_nodes, corner_slot,
@@ -556,6 +566,15 @@
         jnp.transpose(hardening[0], (1, 0, 2)), jnp.transpose(ply_modulus[0], (1, 0, 2)),
         inverse_size, cost_map, migration_plan.reshape(cost_map.shape), block_nodes, corner_slot,
     )
+    results = (disp, vel, moved, hardened)
+    disp, vel, moved, hardened = pl.pallas_call(
+        hand_over,
+        out_shape=tuple(jax.ShapeDtypeStruct(x.shape, f32) for x in results),
+        in_specs=[every] * 4,
+        out_specs=(every,) * 4,
+        scratch_shapes=[dma((3 + kinds,))],
+        compiler_params=pltpu.CompilerParams(vmem_limit_bytes=63 * 1024 * 1024),
+    )(*results)
     return (
         disp.reshape(displacement.shape),
         vel.reshape(displacement.shape),

time: 28.8 us -> 32 us (1.11)
  Pallas kernels: 23.8 us -> 31.2 us
  local copies, waits for them, and re-layouts: 4.14 us -> 0 us
    pallas_call x0 -> x1, Pallas kernels: none -> 7.37 us  [on_device(): pl.pallas_call(hand_over, out_shape=tuple((jax.ShapeDtypeStruct(x.shape,...]
    unnamed x8 -> x0, local copies, waits for them, and re-layouts: 4.14 us -> none
where the time goes in v2:
time: 32 us; the launch traced here: 31.8 us
  Pallas kernels  31.2 us (98%)
  between operations  0.64 us (2%)
    pallas_call x1, Pallas kernels, on_device(): pl.pallas_call(functools.partial(kernel, sizes), out_shape=(jax.ShapeDtyp...  23.8 us
    pallas_call x1, Pallas kernels, on_device(): pl.pallas_call(hand_over, out_shape=tuple((jax.ShapeDtypeStruct(x.shape,...  7.37 us

profile of v2, /device:TPU:0, one launch (start us, length us, event | category | flops | bytes accessed | tf_op | source)
XLA Modules:
  0.0 31.8 jit_solution(11021657409683542633)
XLA Ops:
  0.6 23.8 %shard_map.147 = (f32[40,128]{1,0:T(8,128)}, f32[40,128]{1,0:T(8,128)}, f32[3,5,16,128]{3,2,1,0:T(8,128)}, f32[5,16,128]{2,1,0:T(8,128)}) custom-call(f32[40,128]{1,0:T(8,128)} %bitcast.25, f32[40,128]{1,0:T(8,128)} %bitcast.26, f32[40,128]{1,0:T(8,128)} %bitcast.27, f32[8,128]{1,0:T(8,128)} %bitcast.28, f32[3,5,16,128]{3,2,1,0:T(8,128)} %bitcast.22, ...), custom_call_target="tpu_custom_call" | custom-call | tf_op jit(solution)/shard_map/pallas_call | solution.py:549
  24.4 7.4 %shard_map.148 = (f32[40,128]{1,0:T(8,128)}, f32[40,128]{1,0:T(8,128)}, f32[3,5,16,128]{3,2,1,0:T(8,128)}, f32[5,16,128]{2,1,0:T(8,128)}) custom-call(f32[40,128]{1,0:T(8,128)} %get-tuple-element.12.disp, f32[40,128]{1,0:T(8,128)} %get-tuple-element.13.vel, f32[3,5,16,128]{3,2,1,0:T(8,128)} %get-tuple-element.14.moved, f32[5,16,128]{2,1,0:T(8,128)} %get-tuple-element.15.hardened), custom_call_target="tpu_custom_call" | custom-call | tf_op jit(solution)/shard_map/pallas_call | solution.py:570

commit v3 on v2

--- a/solution.py
+++ b/solution.py
@@ -570,7 +570,7 @@
     disp, vel, moved, hardened = pl.pallas_call(
         hand_over,
         out_shape=tuple(jax.ShapeDtypeStruct(x.shape, f32) for x in results),
-        in_specs=[every] * 4,
+        in_specs=[whole] * 4,
         out_specs=(every,) * 4,
         scratch_shapes=[dma((3 + kinds,))],
         compiler_params=pltpu.CompilerParams(vmem_limit_bytes=63 * 1024 * 1024),

time: 32 us -> 26.3 us (0.82)
  Pallas kernels: 31.2 us -> 25.5 us
    pallas_call x1, Pallas kernels: 7.37 us -> 1.67 us  [on_device(): pl.pallas_call(hand_over, out_shape=tuple((jax.ShapeDtypeStruct(x.shape,...]
where the time goes in v3:
time: 26.3 us; the launch traced here: 26.1 us
  Pallas kernels  25.5 us (97%)
  between operations  0.64 us (2%)
    pallas_call x1, Pallas kernels, on_device(): pl.pallas_call(functools.partial(kernel, sizes), out_shape=(jax.ShapeDtyp...  23.8 us
    pallas_call x1, Pallas kernels, on_device(): pl.pallas_call(hand_over, out_shape=tuple((jax.ShapeDtypeStruct(x.shape,...  1.67 us

profile of v3, /device:TPU:0, one launch (start us, length us, event | category | flops | bytes accessed | tf_op | source)
XLA Modules:
  0.0 26.1 jit_solution(14308102875533348809)
XLA Ops:
  0.6 23.8 %shard_map.147 = (f32[40,128]{1,0:T(8,128)}, f32[40,128]{1,0:T(8,128)}, f32[3,5,16,128]{3,2,1,0:T(8,128)}, f32[5,16,128]{2,1,0:T(8,128)}) custom-call(f32[40,128]{1,0:T(8,128)} %bitcast.25, f32[40,128]{1,0:T(8,128)} %bitcast.26, f32[40,128]{1,0:T(8,128)} %bitcast.27, f32[8,128]{1,0:T(8,128)} %bitcast.28, f32[3,5,16,128]{3,2,1,0:T(8,128)} %bitcast.22, ...), custom_call_target="tpu_custom_call" | custom-call | tf_op jit(solution)/shard_map/pallas_call | solution.py:549
  24.4 1.7 %shard_map.148 = (f32[40,128]{1,0:T(8,128)}, f32[40,128]{1,0:T(8,128)}, f32[3,5,16,128]{3,2,1,0:T(8,128)}, f32[5,16,128]{2,1,0:T(8,128)}) custom-call(f32[40,128]{1,0:T(8,128)} %get-tuple-element.12.disp, f32[40,128]{1,0:T(8,128)} %get-tuple-element.13.vel, f32[3,5,16,128]{3,2,1,0:T(8,128)} %get-tuple-element.14.moved, f32[5,16,128]{2,1,0:T(8,128)} %get-tuple-element.15.hardened), custom_call_target="tpu_custom_call" | custom-call | tf_op jit(solution)/shard_map/pallas_call | solution.py:570

commit v4 on v3

--- a/solution.py
+++ b/solution.py
@@ -31,6 +31,11 @@
 
 def lane_take(x, index):
     return jnp.take_along_axis(x, index, axis=1, mode="promise_in_bounds")
+
+
+def quotient(x, y):
+    guess = pl.reciprocal(y, approx=True)
+    return x * (guess * (2.0 - y * guess))
 
 
 def split_rows(ref_rows, reach):
@@ -283,15 +288,15 @@
             decay = jnp.exp(-RATE * old)
             gap = equal - (YIELD + SATURATE)
             beyond = gap + SATURATE * decay
-            change = beyond / (three + (SATURATE * RATE) * decay)
+            change = quotient(beyond, three + (SATURATE * RATE) * decay)
             yields = beyond > 0.0
             for turn in range(1, NEWTON):
                 decay = jnp.exp(-RATE * (old + change))
                 miss = gap - three * change + SATURATE * decay
-                moved = change + miss / (three + (SATURATE * RATE) * decay)
+                moved = change + quotient(miss, three + (SATURATE * RATE) * decay)
                 change = jnp.where(cost > turn, moved, change)
             change = jnp.where(yields & (cost > 0), change, 0.0)
-            drop = three * change / jnp.maximum(equal, YIELD)
+            drop = quotient(three * change, jnp.maximum(equal, YIELD))
             keep = 1.0 - drop
             harden[g, p] = old + change
             for c in range(3):
@@ -358,9 +363,7 @@
 
     pinned = (station == 0) & (member == 0)
 
-    def forces(step, last):
-        place_windows()
-        elements(0)
+    def outer_sums(step, last):
         sums = assemble(0)
         for i in range(rim_chunks):
             ahead_out[step, :, cut(i)] = sums[own_chunks + i]
@@ -378,7 +381,6 @@
 
         for q in range(chunks):
             partial[:, cut(q)] = sums.get(q, jnp.zeros((ROWS, LANES), jnp.float32))
-        elements(1)
 
     def inner_sums():
         for q, value in assemble(1).items():
@@ -422,14 +424,19 @@
                 disp[:, cut(q)] = place
 
     def one_step(step, carry):
-        forces(step, False)
+        place_windows()
+        elements(0)
+        outer_sums(step, False)
+        elements(1)
         inner_sums()
         finish(step, False)
         return carry
 
     lax.fori_loop(0, STEPS - 1, one_step, 0)
     last = STEPS - 1
-    forces(last, True)
+    place_windows()
+    elements(0)
+    elements(1)
 
     plan_column = jnp.sum(jnp.where(mine, plan_in[...], 0), axis=1, keepdims=True)
     row_at = lax.broadcasted_iota(jnp.int32, (own_blocks, own_blocks), 0)
@@ -475,6 +482,7 @@
     )
     for j in range(1, group):
         move(j).start()
+    outer_sums(last, True)
     stay.start()
     inner_sums()
     finish(last, True)
@@ -549,10 +557,10 @@
     disp, vel, moved, hardened = pl.pallas_call(
         functools.partial(kernel, sizes),
         out_shape=(
-            jax.ShapeDtypeStruct(nodal, f32),
-            jax.ShapeDtypeStruct(nodal, f32),
-            jax.ShapeDtypeStruct((kinds, points, slots_all, size), f32),
-            jax.ShapeDtypeStruct((points, slots_all, size), f32),
+            vmem(nodal, f32),
+            vmem(nodal, f32),
+            vmem((kinds, points, slots_all, size), f32),
+            vmem((points, slots_all, size), f32),
         ),
         in_specs=[every] * 12,
         out_specs=(whole,) * 4,
@@ -569,11 +577,11 @@
     results = (disp, vel, moved, hardened)
     disp, vel, moved, hardened = pl.pallas_call(
         hand_over,
-        out_shape=tuple(jax.ShapeDtypeStruct(x.shape, f32) for x in results),
-        in_specs=[whole] * 4,
+        out_shape=tuple(pltpu.HBM(x.shape, f32) for x in results),
+        in_specs=[pl.BlockSpec(memory_space=pl.ANY)] * 4,
         out_specs=(every,) * 4,
         scratch_shapes=[dma((3 + kinds,))],
-        compiler_params=pltpu.CompilerParams(vmem_limit_bytes=63 * 1024 * 1024),
+        compiler_params=pltpu.CompilerParams(vmem_limit_bytes=1024 * 1024),
     )(*results)
     return (
         disp.reshape(displacement.shape),

time: 26.3 us -> 24 us (0.913)
  Pallas kernels: 25.5 us -> 23.2 us
    pallas_call x2, Pallas kernels: 25.5 us -> 23.2 us  [the longest x1 22.5 us: on_device(): pl.pallas_call(functools.partial(kernel, sizes), out_shape=(vmem(nodal, f...]
where the time goes in v4:
time: 24 us; the launch traced here: 23.8 us
  Pallas kernels  23.2 us (97%)
  between operations  0.64 us (3%)
    pallas_call x1, Pallas kernels, on_device(): pl.pallas_call(functools.partial(kernel, sizes), out_shape=(vmem(nodal, f...  22.5 us
    pallas_call x1, Pallas kernels, on_device(): pl.pallas_call(hand_over, out_shape=tuple((pltpu.HBM(x.shape, f32) for x...  0.73 us

profile of v4, /device:TPU:0, one launch (start us, length us, event | category | flops | bytes accessed | tf_op | source)
XLA Modules:
  0.0 23.8 jit_solution(8143355139510474258)
XLA Ops:
  0.6 22.5 %shard_map.147 = (f32[40,128]{1,0:T(8,128)S(1)}, f32[40,128]{1,0:T(8,128)S(1)}, f32[3,5,16,128]{3,2,1,0:T(8,128)S(1)}, f32[5,16,128]{2,1,0:T(8,128)S(1)}) custom-call(f32[40,128]{1,0:T(8,128)} %bitcast.25, f32[40,128]{1,0:T(8,128)} %bitcast.26, f32[40,128]{1,0:T(8,128)} %bitcast.27, f32[8,128]{1,0:T(8,128)} %bitcast.28, f32[3,5,16,128]{3,2,1,0:T(8,128)} %bitcast.22, ...), custom_call_target="tpu_custom_call" | custom-call | tf_op jit(solution)/shard_map/pallas_call | solution.py:557
  23.1 0.7 %shard_map.148 = (f32[40,128]{1,0:T(8,128)}, f32[40,128]{1,0:T(8,128)}, f32[3,5,16,128]{3,2,1,0:T(8,128)}, f32[5,16,128]{2,1,0:T(8,128)}) custom-call(f32[40,128]{1,0:T(8,128)S(1)} %get-tuple-element.12.disp, f32[40,128]{1,0:T(8,128)S(1)} %get-tuple-element.13.vel, f32[3,5,16,128]{3,2,1,0:T(8,128)S(1)} %get-tuple-element.14.moved, ...), custom_call_target="tpu_custom_call" | custom-call | tf_op jit(solution)/shard_map/pallas_call | solution.py:578
